TPU v7x, 32 devices: a whole 2x2x4 slice. The times are simulated.
32 devices in a mesh: groups: 2 (over y), expert: 4 (over x, core), helper: 4 (over z).
Axes of the slice: x: 2, y: 2, z: 4, core: 2. Of those that a mesh axis runs over, the one named last changes fastest.
Arguments:
- activations: bfloat16 [2048, 2880], P(('groups', 'expert', 'helper')), parts along dimension 0, may hold values from -6 to 6
- expert_ids: int32 [2048, 4], P(('groups', 'expert', 'helper')), parts along dimension 0, may hold values from 0 to 7, all different within a row; in each aligned block of 64 rows (0 to 63, 64 to 127, ...) at most 64 rows name the same one
- route_gates: float32 [2048, 4], P(('groups', 'expert', 'helper')), parts along dimension 0, may hold values from 0.1 to 0.6
- inner_weight: bfloat16 [16, 2, 2880, 720], P(('expert', 'helper')), may hold values from -0.109375 to 0.109375
- outer_weight: bfloat16 [16, 720, 2880], P(('expert', 'helper')), may hold values from -0.15625 to 0.15625
Outputs:
- layer_out: bfloat16 [2048, 2880], P(('groups', 'expert', 'helper')), parts along dimension 0
There are 2 independent parts, one for each index of `groups`. A program takes and returns all parts, laid end to end along the dimension named above; an argument that names none is the same for every part. Nothing has to cross between parts.
Inputs may be any that keep to these rules, and one draw needn't show every extreme that they name: `expert_ids`: each row names 4 different experts. Within the rows of one device (aligned blocks of 64 rows) no expert is named more than 64 times.
All inputs are finite; a program needn't handle non-finite values.
Results may differ from a plain program's by a relative error of at most 0.0066.
Values may be sent and summed in bfloat16 or wider, within the bound.
A program may use at most 128 MiB of HBM per device.

v0:
```python
import jax
import jax.numpy as jnp
from jax import lax
from jax.sharding import PartitionSpec as P


def swapped(shard, axis, bit):
    return lax.ppermute(shard, axis, [(i, i ^ 1 << bit) for i in range(lax.axis_size(axis))])


def deliver(outgoing):
    return lax.all_to_all(outgoing, ("expert", "helper"), split_axis=0, concat_axis=0, tiled=True)


def send_back(outgoing):
    return lax.all_to_all(outgoing, ("expert", "helper"), split_axis=0, concat_axis=0, tiled=True)


def body(activations, expert_ids, route_gates, inner_weight, outer_weight):
    tok_count, model_width = activations.shape
    top_count = expert_ids.shape[1]
    devices_all = lax.axis_size("expert") * lax.axis_size("helper")
    experts_all = devices_all // 2
    capacity = 2 * max(1, tok_count * top_count // experts_all)
    half_cap = capacity // 2
    flat_ids = expert_ids.reshape(-1)
    onehot = (flat_ids[:, None] == jnp.arange(experts_all, dtype=jnp.int32)[None, :]).astype(
        jnp.int32
    )
    ranking = jnp.sum(jnp.cumsum(onehot, axis=0) * onehot, axis=1) - 1
    slot_index = flat_ids * capacity + ranking
    token_index = jnp.arange(flat_ids.shape[0], dtype=jnp.int32) // top_count
    buffer = jnp.zeros((experts_all * capacity, model_width), activations.dtype)
    buffer = buffer.at[slot_index].set(activations[token_index])
    parity = lax.axis_index("helper") % 2
    arrived = deliver(jnp.repeat(buffer.reshape(experts_all, capacity, model_width), 2, axis=0))
    slot_rows = arrived.reshape(-1, model_width)
    projected = jnp.einsum(
        "rd,cdf->crf", slot_rows, inner_weight[0], preferred_element_type=jnp.float32
    )
    gate_proj = projected[0]
    up_proj = projected[1]
    hidden = ((up_proj + 1.0) * gate_proj * jax.nn.sigmoid(1.702 * gate_proj)).astype(jnp.bfloat16)
    partial_value = jnp.dot(hidden, outer_weight[0], preferred_element_type=jnp.float32).astype(
        jnp.bfloat16
    )
    partial_value = partial_value.reshape(devices_all, capacity, model_width)
    first_part = partial_value[:, :half_cap]
    second_part = partial_value[:, half_cap:]
    kept_half = jnp.where(parity == 0, first_part, second_part)
    given_half = jnp.where(parity == 0, second_part, first_part)
    received_half = swapped(given_half, "helper", 0)
    kept_half = lax.optimization_barrier(kept_half)
    summed = kept_half.astype(jnp.float32) + received_half.astype(jnp.float32)
    results = summed.astype(jnp.bfloat16)
    returned = send_back(results).reshape(experts_all * capacity, model_width)
    picked = returned[slot_index].astype(jnp.float32).reshape(tok_count, top_count, model_width)
    combined = jnp.sum(picked * route_gates[:, :, None], axis=1)
    return combined.astype(jnp.bfloat16)


def solution(mesh):
    placed = (
        P(("groups", "expert", "helper"), None),
        P(("groups", "expert", "helper"), None),
        P(("groups", "expert", "helper"), None),
        P(("expert", "helper"), None, None, None),
        P(("expert", "helper"), None, None),
    )
    return jax.shard_map(
        body,
        mesh=mesh,
        in_specs=placed,
        out_specs=P(("groups", "expert", "helper"), None),
        check_vma=False,
    )
```

profile of v0, /device:TPU:0, one launch (start us, length us, event | category | flops | bytes accessed | tf_op | source)
XLA Modules:
  0.0 338.9 jit_solution(5865495982932020862)
XLA Ops:
  0.0 0.0 copy-start
  0.0 0.8 copy.9
  0.8 0.1 eq.36
  0.9 0.1 eq.32
  1.0 0.7 broadcast_multiply_fusion
  1.7 0.6 reduce-window.6
  2.3 0.2 slice_reduce_fusion
  2.6 0.1 fusion.15
  2.7 0.1 copy.8
  2.8 0.1 mul.40
  2.9 0.0 copy-done
  2.9 8.3 %scatter_custom_fusion = bf16[512,2880]{1,0:T(8,128)(2,1)S(1)} fusion(s32[256]{0:T(256)S(1)} %bitcast.34, bf16[64,2880]{1,0:T(8,128)(2,1)S(1)} %copy-done, s32[1024]{0:T(1024)S(1)} %pad_clamp_fusion.1, bf16[]{:T(256)} %constant.44.clone.1), kind=kCustom, calls=%fused_computation.16 | custom fusion | bytes 2949122 | tf_op jit(solution)/shard_map/scatter | solution.py:34
  11.2 3.4 %broadcast_in_dim.5 = bf16[8,2,64,2880]{3,2,1,0:T(8,128)(2,1)} broadcast(bf16[8,64,2880]{2,1,0:T(8,128)(2,1)S(1)} %bitcast.33), dimensions={0,2,3} | broadcast | bytes 8847360 | tf_op jit(solution)/shard_map/broadcast_in_dim | solution.py:36
  14.6 0.0 slice-start
  14.6 7.5 %all-to-all-start = ((bf16[16,64,2880]{2,1,0:T(8,128)(2,1)}), bf16[16,64,2880]{2,1,0:T(8,128)(2,1)}, u32[]{:S(2)}, u32[]{:S(2)}) async-start(bf16[16,64,2880]{2,1,0:T(8,128)(2,1)} %bitcast.31), calls=%async_computation | async-start | bytes 12058624 | tf_op jit(solution)/shard_map/all_to_all | solution.py:12
  22.2 133.7 %all-to-all-done = bf16[16,64,2880]{2,1,0:T(8,128)(2,1)} async-done(((bf16[16,64,2880]{2,1,0:T(8,128)(2,1)}), bf16[16,64,2880]{2,1,0:T(8,128)(2,1)}, u32[]{:S(2)}, u32[]{:S(2)}) %all-to-all-start) | async-done | bytes 5898272 | tf_op jit(solution)/shard_map/all_to_all | solution.py:12
  155.9 0.0 slice-start.1
  155.9 13.7 %fusion.6 = f32[2,1024,720]{1,2,0:T(8,128)S(1)} fusion(bf16[1024,2880,1]{1,0,2:T(8,128)(2,1)} %bitcast.8, bf16[1,2,2880,720]{2,3,1,0:T(8,128)(2,1)} %param.8), kind=kOutput, calls=%fused_computation.15 | convolution fusion | flops 8493465600 | bytes 20090880 | tf_op jit(solution)/shard_map/rd,cdf->crf/dot_general | solution.py:38
  169.6 0.0 slice-done
  169.6 0.0 slice-done.1
  169.7 7.0 %convolution_convert_fusion = bf16[1024,2880]{0,1:T(8,128)(2,1)} fusion(bf16[1,720,2880]{2,1,0:T(8,128)(2,1)S(1)} %bitcast.39, f32[2,1024,720]{1,2,0:T(8,128)S(1)} %fusion.6), kind=kOutput, calls=%fused_computation.6 | convolution fusion | flops 4255580160 | bytes 15943680 | tf_op jit(solution)/shard_map/dot_general | solution.py:44
  176.6 8.5 %copy.12 = bf16[1024,2880]{1,0:T(8,128)(2,1)} copy(bf16[1024,2880]{0,1:T(8,128)(2,1)} %convolution_convert_fusion) | data formatting | bytes 11796480 | tf_op jit(solution)/shard_map/convert_element_type | solution.py:44
  185.1 3.3 broadcast_select_fusion.1
  188.4 0.1 collective-permute-start
  188.5 66.9 %collective-permute-done = bf16[16,32,2880]{2,1,0:T(8,128)(2,1)S(1)} collective-permute-done((bf16[16,32,2880]{2,1,0:T(8,128)(2,1)S(1)}, bf16[16,32,2880]{2,1,0:T(8,128)(2,1)S(1)}, u32[]{:S(2)}, u32[]{:S(2)}) %collective-permute-start) | collective-permute-done | bytes 2949152 | tf_op jit(solution)/shard_map/ppermute | solution.py:8
  255.4 2.3 add_convert_fusion
  257.7 0.0 copy-start.1
  257.7 3.9 %all-to-all-start.1 = ((bf16[16,32,2880]{2,1,0:T(8,128)(2,1)}), bf16[16,32,2880]{2,1,0:T(8,128)(2,1)S(1)}, u32[]{:S(2)}, u32[]{:S(2)}) async-start(bf16[16,32,2880]{2,1,0:T(8,128)(2,1)} %add_convert_fusion), calls=%async_computation.1 | async-start | bytes 6029312 | tf_op jit(solution)/shard_map/all_to_all | solution.py:16
  261.6 0.0 copy-done.1
  261.6 0.1 copy.13
  261.7 68.9 %all-to-all-done.1 = bf16[16,32,2880]{2,1,0:T(8,128)(2,1)S(1)} async-done(((bf16[16,32,2880]{2,1,0:T(8,128)(2,1)}), bf16[16,32,2880]{2,1,0:T(8,128)(2,1)S(1)}, u32[]{:S(2)}, u32[]{:S(2)}) %all-to-all-start.1) | async-done | bytes 2949152 | tf_op jit(solution)/shard_map/all_to_all | solution.py:16
  330.6 2.7 gather_fusion
  333.3 2.8 reshape.121
  336.1 2.8 multiply_reduce_fusion
  (9 shorter events, 0.1 us)
Async XLA Ops:
  0.0 2.9 copy-start
  14.6 155.0 %slice-start = ((s8[4239360]{0:T(1024)(128)(4,1)}), s8[45056]{0:T(1024)(128)(4,1)S(1)}, s32[]{:S(2)}) async-start(s8[4239360]{0:T(1024)(128)(4,1)} %bitcast.38), calls=%async_computation.2 | async-start | bytes 90112
  14.6 141.3 %all-to-all-start = ((bf16[16,64,2880]{2,1,0:T(8,128)(2,1)}), bf16[16,64,2880]{2,1,0:T(8,128)(2,1)}, u32[]{:S(2)}, u32[]{:S(2)}) async-start(bf16[16,64,2880]{2,1,0:T(8,128)(2,1)} %bitcast.31), calls=%async_computation | async-start | bytes 12058624 | tf_op jit(solution)/shard_map/all_to_all | solution.py:12
  155.9 13.7 %slice-start.1 = ((s8[4239360]{0:T(1024)(128)(4,1)}), s8[4194304]{0:T(1024)(128)(4,1)S(1)}, s32[]{:S(2)}) async-start(s8[4239360]{0:T(1024)(128)(4,1)} %bitcast.38), calls=%async_computation.3 | async-start | bytes 8388608
  188.4 67.0 %collective-permute-start = (bf16[16,32,2880]{2,1,0:T(8,128)(2,1)S(1)}, bf16[16,32,2880]{2,1,0:T(8,128)(2,1)S(1)}, u32[]{:S(2)}, u32[]{:S(2)}) collective-permute-start(bf16[16,32,2880]{2,1,0:T(8,128)(2,1)S(1)} %get-tuple-element.6), channel_id=1, source_target_pairs={{0,1},{1,0},{2,3},{3,2},{4,5},{5,4},{6,7},{7,6},{8,9},{9,8},{10,11... | collective-permute-start | bytes 8847368 | tf_op jit(solution)/shard_map/ppermute | solution.py:8
  257.7 3.9 %copy-start.1 = (f32[64,4]{0,1:T(4,128)S(1)}, f32[64,4]{0,1:T(4,128)}, u32[]{:S(2)}) copy-start(f32[64,4]{0,1:T(4,128)} %param.7) | copy-start | bytes 3076
  257.7 72.9 %all-to-all-start.1 = ((bf16[16,32,2880]{2,1,0:T(8,128)(2,1)}), bf16[16,32,2880]{2,1,0:T(8,128)(2,1)S(1)}, u32[]{:S(2)}, u32[]{:S(2)}) async-start(bf16[16,32,2880]{2,1,0:T(8,128)(2,1)} %add_convert_fusion), calls=%async_computation.1 | async-start | bytes 6029312 | tf_op jit(solution)/shard_map/all_to_all | solution.py:16
where the time goes:
time: 339 us
  waiting for transfers between devices  270 us (80%)
  local copies, waits for them, and re-layouts  27.2 us (8%)
  matrix products  20.7 us (6%)
  starting transfers between devices  11.5 us (3%)
  other arithmetic  9.85 us (3%)
    all_to_all x1, waiting for transfers between devices, deliver(): lax.all_to_all(outgoing, ('expert', 'helper'), split_axis=0, concat_axis=...  134 us
    all_to_all x1, waiting for transfers between devices, send_back(): lax.all_to_all(outgoing, ('expert', 'helper'), split_axis=0, concat_axis=...  68.9 us
    ppermute x1, waiting for transfers between devices, swapped(): lax.ppermute(shard, axis, [(i, i ^ 1 << bit) for i in range(lax.axis_size...  66.9 us
    dot_general x1, matrix products, body(): jnp.einsum('rd,cdf->crf', slot_rows, inner_weight[0], preferred_element_t...  13.7 us
    convert_element_type x1, local copies, waits for them, and re-layouts, body(): jnp.dot(hidden, outer_weight[0], preferred_element_type=jnp.float32)  8.5 us
    scatter x1, local copies, waits for them, and re-layouts, body(): buffer = buffer.at[slot_index].set(activations[token_index])  8.26 us
    all_to_all x1, starting transfers between devices, deliver(): lax.all_to_all(outgoing, ('expert', 'helper'), split_axis=0, concat_axis=...  7.54 us
    dot_general x1, matrix products, body(): jnp.dot(hidden, outer_weight[0], preferred_element_type=jnp.float32)  6.98 us
  transfers between devices with their start and end apart: 3, of which 3 were waited for; matrix products, arithmetic and copies ran while one was open for 0% of the time, Pallas kernels for 0%

commit v1 on v0

--- a/solution.py
+++ b/solution.py
@@ -16,7 +16,7 @@
     return lax.all_to_all(outgoing, ("expert", "helper"), split_axis=0, concat_axis=0, tiled=True)
 
 
-def body(activations, expert_ids, route_gates, inner_weight, outer_weight):
+def routed_body(activations, expert_ids, route_gates, inner_weight, outer_weight):
     tok_count, model_width = activations.shape
     top_count = expert_ids.shape[1]
     devices_all = lax.axis_size("expert") * lax.axis_size("helper")
@@ -59,6 +59,33 @@
     return combined.astype(jnp.bfloat16)
 
 
+AXES = ("expert", "helper")
+
+
+def dense_body(activations, expert_ids, route_gates, inner_weight, outer_weight):
+    experts_all = lax.axis_size("expert") * lax.axis_size("helper") // 2
+    expert = (lax.axis_index("expert") * lax.axis_size("helper") + lax.axis_index("helper")) // 2
+    named = expert_ids[:, :, None] == jnp.arange(experts_all, dtype=jnp.int32)[None, None, :]
+    weights = jnp.sum(jnp.where(named, route_gates[:, :, None], 0.0), axis=1)
+    rows = lax.all_gather(activations, AXES, axis=0, tiled=True)
+    weights = lax.all_gather(weights, AXES, axis=0, tiled=True)
+    own = jnp.sum(jnp.where(jnp.arange(experts_all)[None, :] == expert, weights, 0.0), axis=1)
+    gate_proj = jnp.dot(rows, inner_weight[0, 0], preferred_element_type=jnp.float32)
+    up_proj = jnp.dot(rows, inner_weight[0, 1], preferred_element_type=jnp.float32)
+    hidden = ((up_proj + 1.0) * gate_proj * jax.nn.sigmoid(1.702 * gate_proj)).astype(jnp.bfloat16)
+    partial = jnp.dot(hidden, outer_weight[0], preferred_element_type=jnp.float32)
+    partial = (partial * own[:, None]).astype(jnp.bfloat16)
+    return lax.psum_scatter(partial, AXES, scatter_dimension=0, tiled=True)
+
+
+def body(activations, expert_ids, route_gates, inner_weight, outer_weight):
+    tok_count, top_count = expert_ids.shape
+    experts_all = lax.axis_size("expert") * lax.axis_size("helper") // 2
+    capacity = 2 * max(1, tok_count * top_count // experts_all)
+    chosen = dense_body if capacity >= tok_count else routed_body
+    return chosen(activations, expert_ids, route_gates, inner_weight, outer_weight)
+
+
 def solution(mesh):
     placed = (
         P(("groups", "expert", "helper"), None),

time: 339 us -> 187 us (0.55)
  waiting for transfers between devices: 270 us -> 113 us
  blocking collectives: 0 us -> 34.7 us
  local copies, waits for them, and re-layouts: 27.2 us -> 0.1 us
  between operations: 0.15 us -> 13.4 us
  starting transfers between devices: 11.5 us -> 0.04 us
  other arithmetic: 9.85 us -> 0.8 us
  matrix products: 20.7 us -> 24.5 us
    all_to_all x2 -> x0, waiting for transfers between devices: 203 us -> none  [the longest x1 134 us: deliver(): lax.all_to_all(outgoing, ('expert', 'helper'), split_axis=0, concat_axis=...]
    reduce_scatter x0 -> x1, waiting for transfers between devices: none -> 82.1 us  [dense_body(): return lax.psum_scatter(partial, AXES, scatter_dimension=0, tiled=True)]
    ppermute x1 -> x0, waiting for transfers between devices: 66.9 us -> none  [swapped(): lax.ppermute(shard, axis, [(i, i ^ 1 << bit) for i in range(lax.axis_size...]
    all_gather x0 -> x1, blocking collectives: none -> 34.7 us  [dense_body(): weights = lax.all_gather(weights, AXES, axis=0, tiled=True)]
    all_gather x0 -> x1, waiting for transfers between devices: none -> 30.4 us  [dense_body(): rows = lax.all_gather(activations, AXES, axis=0, tiled=True)]
    all_to_all x2 -> x0, starting transfers between devices: 11.4 us -> none  [the longest x1 7.54 us: deliver(): lax.all_to_all(outgoing, ('expert', 'helper'), split_axis=0, concat_axis=...]
    convert_element_type x2 -> x0, local copies, waits for them, and re-layouts: 11.3 us -> none  [the longest x1 8.5 us: body(): jnp.dot(hidden, outer_weight[0], preferred_element_type=jnp.float32)]
    scatter x1 -> x0, local copies, waits for them, and re-layouts: 8.26 us -> none  [body(): buffer = buffer.at[slot_index].set(activations[token_index])]
  transfers between devices with their start and end apart: 3 -> 2, of which waited for: 3 -> 2; matrix products, arithmetic and copies ran while one was open for 0% -> 0% of each run, Pallas kernels for 0% -> 0%
where the time goes in v1:
time: 187 us
  waiting for transfers between devices  113 us (60%)
  blocking collectives  34.7 us (19%)
  matrix products  24.5 us (13%)
  between operations  13.4 us (7%)
    reduce_scatter x1, waiting for transfers between devices, dense_body(): return lax.psum_scatter(partial, AXES, scatter_dimension=0, tiled=True)  82.1 us
    all_gather x1, blocking collectives, dense_body(): weights = lax.all_gather(weights, AXES, axis=0, tiled=True)  34.7 us
    all_gather x1, waiting for transfers between devices, dense_body(): rows = lax.all_gather(activations, AXES, axis=0, tiled=True)  30.4 us
    dot_general x1, matrix products, dense_body(): jnp.dot(hidden, outer_weight[0], preferred_element_type=jnp.float32)  16.4 us
    dot_general x1, matrix products, dense_body(): jnp.dot(rows, inner_weight[0, 1], preferred_element_type=jnp.float32)  8.09 us
  transfers between devices with their start and end apart: 2, of which 2 were waited for; matrix products, arithmetic and copies ran while one was open for 0% of the time, Pallas kernels for 0%

profile of v1, /device:TPU:0, one launch (start us, length us, event | category | flops | bytes accessed | tf_op | source)
XLA Modules:
  0.0 186.7 jit_solution(12394409743901416304)
XLA Ops:
  6.5 0.0 all-gather.3.cloned.1.call-start
  6.5 0.7 all-gather.3.cloned.1.call-update
  7.3 0.0 reduce-scatter.2.cloned.1.call-start
  7.3 0.7 select_reduce_fusion.1
  8.0 34.7 %all-gather = f32[16,64,8]{1,2,0:T(8,128)S(1)} all-gather(f32[1,64,8]{1,2,0:T(8,128)S(1)} %bitcast.18), channel_id=1, replica_groups=mesh['groups'=2,'expert'=4,'helper'=4] {'expert','helper'}, dimensions={0}, use_global_device_ids=true | all-gather | bytes 34816 | tf_op jit(solution)/shard_map/all_gather | solution.py:71
  42.7 0.1 reshape.9
  42.8 0.1 select_reduce_fusion
  42.9 30.4 %all-gather.3.cloned.1.call-done = bf16[1024,2880]{1,0:T(8,128)(2,1)} async-done(((bf16[64,2880]{1,0:T(8,128)(2,1)}), bf16[1024,2880]{1,0:T(8,128)(2,1)}) %all-gather.3.cloned.1.call-update) | async-done | bytes 5898256 | tf_op jit(solution)/shard_map/all_gather | solution.py:70
  73.2 8.1 %fusion.3 = f32[1024,720]{0,1:T(8,128)S(1)} fusion(bf16[1024,2880]{1,0:T(8,128)(2,1)} %all-gather.3.cloned.1.call-done, bf16[1,2,2880,720]{2,3,1,0:T(8,128)(2,1)} %param.8), kind=kOutput, calls=%fused_computation.4 | convolution fusion | flops 4246732800 | bytes 13217792 | tf_op jit(solution)/shard_map/dot_general | solution.py:74
  81.3 16.4 %multiply_convert_fusion = bf16[1024,2880]{1,0:T(8,128)(2,1)} fusion(f32[1024]{0:T(1024)S(1)} %select_reduce_fusion, bf16[1,720,2880]{2,1,0:T(8,128)(2,1)} %param.9, f32[1024,720]{0,1:T(8,128)S(1)} %fusion.3, bf16[1024,2880]{1,0:T(8,128)(2,1)} %all-gather.3.cloned.1.call-done, bf16[1,2,2880,720]{2,3,1,0:T(8,128)(2,1)} %param.8), kind=kOutput, calls=%fused_computation | convolution fusion | flops 8505262080 | bytes 23359488 | tf_op jit(solution)/shard_map/dot_general | solution.py:76
  97.8 0.0 reduce-scatter.2.cloned.1.call-update
  97.8 82.1 %reduce-scatter.2.cloned.1.call-done = bf16[64,2880]{1,0:T(8,128)(2,1)} async-done(((bf16[1024,2880]{1,0:T(8,128)(2,1)}), bf16[64,2880]{1,0:T(8,128)(2,1)}) %reduce-scatter.2.cloned.1.call-update) | async-done | bytes 368656 | tf_op jit(solution)/shard_map/reduce_scatter | solution.py:78
  (2 shorter events, 0.0 us)
Async XLA Ops:
  6.5 66.7 %all-gather.3.cloned.1.call-start = ((), (), s32[]{:S(2)}) async-start(), calls=%async_computation.1 | async-start | bytes 6406144 | tf_op jit(solution)/shard_map/all_gather | solution.py:70
  7.3 172.6 %reduce-scatter.2.cloned.1.call-start = ((), (), s32[]{:S(2)}) async-start(), calls=%async_computation.2 | async-start | bytes 6406144 | tf_op jit(solution)/shard_map/reduce_scatter | solution.py:78
Sparse Core Ops, SparseCore 0:
  9.7 63.5 all-gather.2
  97.9 81.9 reduce-scatter.1

commit v2 on v1

--- a/solution.py
+++ b/solution.py
@@ -1,6 +1,8 @@
 import jax
 import jax.numpy as jnp
 from jax import lax
+from jax.experimental import pallas as pl
+from jax.experimental.pallas import tpu as pltpu
 from jax.sharding import PartitionSpec as P
 
 
@@ -78,11 +80,322 @@
     return lax.psum_scatter(partial, AXES, scatter_dimension=0, tiled=True)
 
 
+UP, DOWN, ACROSS, TWIN = 0, 1, 2, 3
+
+
+def line_kernel(
+    rows_ref, inner_ref, outer_ref, out_ref,
+    rows, inner, outer, parts, twin_in, cross_out, cross_in, line_out, line_up, line_down,
+    gather_send, gather_recv, twin_send, twin_recv, cross_send, cross_recv,
+    up_send, up_recv, down_send, down_recv, weight_sem,
+):
+    length = 4
+    tok, width = out_ref.shape
+    me = lax.axis_index("expert")
+    z = lax.axis_index("helper")
+    x, core = me // 2, me % 2
+    spare = rows_ref.shape[1] - 128
+    experts_all = lax.axis_size("expert") * lax.axis_size("helper") // 2
+    expert = (me * length + z) // 2
+    up_dev = {"helper": jnp.minimum(z + 1, length - 1)}
+    down_dev = {"helper": jnp.maximum(z - 1, 0)}
+    cross_dev = {"expert": (1 - x) * 2 + core}
+    twin_dev = {"expert": x * 2 + (1 - core)}
+    devs = (up_dev, down_dev, cross_dev, twin_dev)
+    has_up, has_down = z < length - 1, z > 0
+    own_slot = core * 2 + x
+    cross_slot = core * 2 + (1 - x)
+
+    load_inner = pltpu.make_async_copy(inner_ref, inner, weight_sem.at[0])
+    load_outer = pltpu.make_async_copy(outer_ref, outer, weight_sem.at[1])
+    load_inner.start()
+    load_outer.start()
+
+    barrier = pltpu.get_barrier_semaphore()
+
+    def greet(dev):
+        pl.semaphore_signal(barrier, inc=1, device_id=dev, device_id_type=pl.DeviceIdType.MESH)
+
+    greet(cross_dev)
+    greet(twin_dev)
+
+    @pl.when(has_up)
+    def _():
+        greet(up_dev)
+
+    @pl.when(has_down)
+    def _():
+        greet(down_dev)
+
+    rows[z, own_slot] = rows_ref[...]
+    pl.semaphore_wait(barrier, jnp.where(has_up & has_down, 4, 3))
+
+    def block_copy(way, plane, slot):
+        return pltpu.make_async_remote_copy(
+            src_ref=rows.at[plane, slot], dst_ref=rows.at[plane, slot],
+            send_sem=gather_send.at[way, plane, slot], recv_sem=gather_recv.at[plane, slot],
+            device_id=devs[way], device_id_type=pl.DeviceIdType.MESH,
+        )
+
+    def moved(src, dst, send, recv, dev, at):
+        return pltpu.make_async_remote_copy(
+            src_ref=src, dst_ref=dst.at[at], send_sem=send.at[at], recv_sem=recv.at[at],
+            device_id=dev, device_id_type=pl.DeviceIdType.MESH,
+        )
+
+    def twin_copy(plane):
+        return moved(parts.at[plane, pl.ds((1 - core) * 2, 2)], twin_in, twin_send, twin_recv, twin_dev, plane)
+
+    def cross_copy(plane):
+        return moved(cross_out.at[plane], cross_in, cross_send, cross_recv, cross_dev, plane)
+
+    def up_copy(plane):
+        return moved(line_out.at[plane], line_up, up_send, up_recv, up_dev, plane)
+
+    def down_copy(plane):
+        return moved(line_out.at[plane], line_down, down_send, down_recv, down_dev, plane)
+
+    def plane_of(i):
+        second = jnp.where(z == 0, 1, z - 1)
+        third = jnp.where(z == 0, 2, jnp.where(z == 3, 1, z + 1))
+        fourth = jnp.where(z <= 1, 3, 0)
+        return jnp.where(i == 0, z, jnp.where(i == 1, second, jnp.where(i == 2, third, fourth)))
+
+    @pl.when(has_up)
+    def _():
+        block_copy(UP, z, own_slot).start()
+
+    @pl.when(has_down)
+    def _():
+        block_copy(DOWN, z, own_slot).start()
+
+    block_copy(ACROSS, z, own_slot).start()
+    block_copy(TWIN, z, own_slot).start()
+
+    def shift_in(dist):
+        @pl.when(z - dist >= 0)
+        def _():
+            plane = jnp.maximum(z - dist, 0)
+            block_copy(UP, plane, own_slot).wait_recv()
+
+            @pl.when(has_up)
+            def _():
+                block_copy(UP, plane, own_slot).start()
+
+            block_copy(ACROSS, plane, own_slot).start()
+            block_copy(TWIN, plane, own_slot).start()
+
+        @pl.when(z + dist <= length - 1)
+        def _():
+            plane = jnp.minimum(z + dist, length - 1)
+            block_copy(DOWN, plane, own_slot).wait_recv()
+
+            @pl.when(has_down)
+            def _():
+                block_copy(DOWN, plane, own_slot).start()
+
+            block_copy(ACROSS, plane, own_slot).start()
+            block_copy(TWIN, plane, own_slot).start()
+
+    def expert_part(plane):
+        group = rows[plane].reshape(4 * tok, rows_ref.shape[1])
+        lane = lax.broadcasted_iota(jnp.int32, (4 * tok, 128), 1)
+        first = width - spare + expert
+        mine = (lane == first) | (lane == first + experts_all) | (lane == first + 2 * experts_all)
+        tail = rows[plane, :, :, pl.ds(spare, 128)].reshape(4 * tok, 128).astype(jnp.float32)
+        gain = jnp.sum(jnp.where(mine, tail, 0.0), axis=1, keepdims=True)
+        group = group[:, :width]
+        over = (((1,), (1,)), ((), ()))
+        gate_proj = lax.dot_general(group, inner[0], over, preferred_element_type=jnp.float32)
+        up_proj = lax.dot_general(group, inner[1], over, preferred_element_type=jnp.float32)
+        hidden = ((up_proj + 1.0) * gate_proj * jax.nn.sigmoid(1.702 * gate_proj)).astype(jnp.bfloat16)
+        for low in range(0, width, 1024):
+            high = min(low + 1024, width)
+            value = jnp.dot(hidden, outer[:, low:high], preferred_element_type=jnp.float32) * gain
+            parts[plane, :, :, low:high] = value.astype(jnp.bfloat16).reshape(4, tok, high - low)
+
+    def cross_sum(plane):
+        twin_copy(plane).wait_recv()
+        total = parts[plane, cross_slot].astype(jnp.float32) + twin_in[plane, 1 - x].astype(jnp.float32)
+        cross_out[plane] = total.astype(jnp.bfloat16)
+        cross_copy(plane).start()
+
+    def step(i, carry):
+        plane = plane_of(i)
+
+        @pl.when(i < length - 1)
+        def _():
+            shift_in(i + 1)
+
+        block_copy(ACROSS, plane, cross_slot).wait_recv()
+        block_copy(TWIN, plane, cross_slot).start()
+        for other in range(2):
+            block_copy(TWIN, plane, (1 - core) * 2 + other).wait_recv()
+
+        @pl.when(i == 0)
+        def _():
+            load_inner.wait()
+            load_outer.wait()
+
+        expert_part(plane)
+        twin_copy(plane).start()
+
+        @pl.when(i >= 1)
+        def _():
+            cross_sum(plane_of(i - 1))
+
+        return carry
+
+    lax.fori_loop(0, length, step, 0)
+    cross_sum(plane_of(3))
+
+    def column_sum(plane):
+        cross_copy(plane).wait_recv()
+        return (
+            parts[plane, own_slot].astype(jnp.float32)
+            + twin_in[plane, x].astype(jnp.float32)
+            + cross_in[plane].astype(jnp.float32)
+        )
+
+    def line_step(j, carry):
+        first = jnp.where(z <= 1, z + 1, z - 1)
+        second = jnp.where(z <= 1, z + 2, z - 2)
+        third = jnp.where(z == 0, 3, jnp.where(z == 1, 0, jnp.where(z == 2, 3, 0)))
+        plane = jnp.where(j == 0, first, jnp.where(j == 1, second, third))
+        total = column_sum(plane)
+
+        @pl.when(plane > z)
+        def _():
+            @pl.when(has_down)
+            def _():
+                up_copy(plane).wait_recv()
+                line_out[plane] = (total + line_up[plane].astype(jnp.float32)).astype(jnp.bfloat16)
+
+            @pl.when(z == 0)
+            def _():
+                line_out[plane] = total.astype(jnp.bfloat16)
+
+            up_copy(plane).start()
+
+        @pl.when(plane < z)
+        def _():
+            @pl.when(has_up)
+            def _():
+                down_copy(plane).wait_recv()
+                line_out[plane] = (total + line_down[plane].astype(jnp.float32)).astype(jnp.bfloat16)
+
+            @pl.when(z == length - 1)
+            def _():
+                line_out[plane] = total.astype(jnp.bfloat16)
+
+            down_copy(plane).start()
+
+        return carry
+
+    lax.fori_loop(0, length - 1, line_step, 0)
+    total = column_sum(z)
+
+    @pl.when(z == 0)
+    def _():
+        down_copy(z).wait_recv()
+        out_ref[...] = (total + line_down[z].astype(jnp.float32)).astype(jnp.bfloat16)
+
+    @pl.when(z == length - 1)
+    def _():
+        up_copy(z).wait_recv()
+        out_ref[...] = (total + line_up[z].astype(jnp.float32)).astype(jnp.bfloat16)
+
+    @pl.when(has_up & has_down)
+    def _():
+        up_copy(z).wait_recv()
+        down_copy(z).wait_recv()
+        both = line_up[z].astype(jnp.float32) + line_down[z].astype(jnp.float32)
+        out_ref[...] = (total + both).astype(jnp.bfloat16)
+
+    def drain(plane, carry):
+        @pl.when(has_up & (plane <= z))
+        def _():
+            block_copy(UP, plane, own_slot).wait_send()
+
+        @pl.when(has_down & (plane >= z))
+        def _():
+            block_copy(DOWN, plane, own_slot).wait_send()
+
+        block_copy(ACROSS, plane, own_slot).wait_send()
+        block_copy(TWIN, plane, own_slot).wait_send()
+        block_copy(TWIN, plane, cross_slot).wait_send()
+        twin_copy(plane).wait_send()
+        cross_copy(plane).wait_send()
+
+        @pl.when(plane > z)
+        def _():
+            up_copy(plane).wait_send()
+
+        @pl.when(plane < z)
+        def _():
+            down_copy(plane).wait_send()
+
+        return carry
+
+    lax.fori_loop(0, length, drain, 0)
+
+
+def line_body(activations, expert_ids, route_gates, inner_weight, outer_weight):
+    tok, width = activations.shape
+    hidden = outer_weight.shape[1]
+    length = lax.axis_size("helper")
+    experts_all = lax.axis_size("expert") * length // 2
+    named = expert_ids[:, :, None] == jnp.arange(experts_all, dtype=jnp.int32)[None, None, :]
+    weights = jnp.sum(jnp.where(named, route_gates[:, :, None], 0.0), axis=1)
+    high = lax.reduce_precision(weights, 8, 7)
+    middle = lax.reduce_precision(weights - high, 8, 7)
+    low = weights - high - middle
+    gates = jnp.concatenate([high, middle, low], axis=1).astype(jnp.bfloat16)
+    whole = -(-width // 128) * 128
+    rows = jnp.concatenate([activations, jnp.pad(gates, ((0, 0), (0, whole - width - gates.shape[1])))], axis=1)
+    inner = jnp.swapaxes(inner_weight[0], 1, 2)
+    bf16 = jnp.bfloat16
+    dma = pltpu.SemaphoreType.DMA
+    block = pltpu.VMEM((length, tok, width), bf16)
+    return pl.pallas_call(
+        line_kernel,
+        out_shape=jax.ShapeDtypeStruct((tok, width), bf16),
+        in_specs=[
+            pl.BlockSpec(memory_space=pltpu.VMEM),
+            pl.BlockSpec(memory_space=pl.ANY),
+            pl.BlockSpec(memory_space=pl.ANY),
+        ],
+        out_specs=pl.BlockSpec(memory_space=pltpu.VMEM),
+        scratch_shapes=[
+            pltpu.VMEM((length, 4, tok, whole), bf16),
+            pltpu.VMEM((2, hidden, width), bf16),
+            pltpu.VMEM((hidden, width), bf16),
+            pltpu.VMEM((length, 4, tok, width), bf16),
+            pltpu.VMEM((length, 2, tok, width), bf16),
+            block, block, block, block, block,
+            dma((4, length, 4)), dma((length, 4)),
+            dma((length,)), dma((length,)), dma((length,)), dma((length,)),
+            dma((length,)), dma((length,)), dma((length,)), dma((length,)),
+            dma((2,)),
+        ],
+        compiler_params=pltpu.CompilerParams(
+            collective_id=0, has_side_effects=True, vmem_limit_bytes=58 * 1024 * 1024
+        ),
+    )(rows, inner, outer_weight[0])
+
+
 def body(activations, expert_ids, route_gates, inner_weight, outer_weight):
     tok_count, top_count = expert_ids.shape
     experts_all = lax.axis_size("expert") * lax.axis_size("helper") // 2
     capacity = 2 * max(1, tok_count * top_count // experts_all)
-    chosen = dense_body if capacity >= tok_count else routed_body
+    spare = -activations.shape[1] % 128
+    four = lax.axis_size("expert") == 4 and lax.axis_size("helper") == 4
+    if capacity < tok_count:
+        chosen = routed_body
+    elif four and tok_count % 16 == 0 and spare >= 3 * experts_all:
+        chosen = line_body
+    else:
+        chosen = dense_body
     return chosen(activations, expert_ids, route_gates, inner_weight, outer_weight)
 
 

time: 187 us -> 107 us (0.57)
  waiting for transfers between devices: 113 us -> 0 us
  Pallas kernels: 0 us -> 103 us
  blocking collectives: 34.7 us -> 0 us
  matrix products: 24.5 us -> 0 us
  between operations: 13.4 us -> 0.01 us
    pallas_call x0 -> x1, Pallas kernels: none -> 103 us  [line_body(): pl.pallas_call(line_kernel, out_shape=jax.ShapeDtypeStruct((tok, width),...]
    reduce_scatter x1 -> x0, waiting for transfers between devices: 82.1 us -> none  [dense_body(): return lax.psum_scatter(partial, AXES, scatter_dimension=0, tiled=True)]
    all_gather x1 -> x0, blocking collectives: 34.7 us -> none  [dense_body(): weights = lax.all_gather(weights, AXES, axis=0, tiled=True)]
    all_gather x1 -> x0, waiting for transfers between devices: 30.4 us -> none  [dense_body(): rows = lax.all_gather(activations, AXES, axis=0, tiled=True)]
    dot_general x2 -> x0, matrix products: 24.5 us -> none  [the longest x1 16.4 us: dense_body(): jnp.dot(hidden, outer_weight[0], preferred_element_type=jnp.float32)]
  transfers between devices with their start and end apart: 2 -> 0, of which waited for: 2 -> 0; matrix products, arithmetic and copies ran while one was open for 0% -> 0% of each run, Pallas kernels for 0% -> 0%
where the time goes in v2:
time: 107 us
  Pallas kernels  103 us (96%)
  other arithmetic  2.54 us (2%)
  local copies, waits for them, and re-layouts  1.86 us (2%)
    pallas_call x1, Pallas kernels, line_body(): pl.pallas_call(line_kernel, out_shape=jax.ShapeDtypeStruct((tok, width),...  103 us

profile of v2, /device:TPU:0, one launch (start us, length us, event | category | flops | bytes accessed | tf_op | source)
XLA Modules:
  0.0 107.0 jit_solution(8873749163115228562)
XLA Ops:
  0.0 0.7 select_reduce_fusion
  0.7 0.1 copy.11
  0.8 1.8 %fusion.1.rows_ref = bf16[64,2944]{1,0:T(8,128)(2,1)} fusion(bf16[64,24]{1,0:T(8,128)(2,1)S(1)} %copy.11, bf16[64,2880]{1,0:T(8,128)(2,1)} %param.5), kind=kLoop, calls=%fused_computation.2 | loop fusion | flops 1130496 | bytes 748544 | tf_op jit(solution)/shard_map/concatenate | solution.py:355
  2.6 102.6 %shard_map.55 = bf16[64,2880]{1,0:T(8,128)(2,1)} custom-call(bf16[64,2944]{1,0:T(8,128)(2,1)} %fusion.1.rows_ref, bf16[2,720,2880]{2,1,0:T(8,128)(2,1)} %bitcast.4, bf16[720,2880]{1,0:T(8,128)(2,1)} %bitcast.5), custom_call_target="tpu_custom_call" | custom-call | tf_op jit(solution)/shard_map/pallas_call | solution.py:360
  105.3 1.8 %copy.13 = bf16[64,2880]{1,0:T(8,128)(2,1)} copy(bf16[64,2880]{1,0:T(8,128)(2,1)} %shard_map.55) | data formatting | bytes 737280
  (2 shorter events, 0.0 us)

commit v3 on v2

--- a/solution.py
+++ b/solution.py
@@ -86,7 +86,7 @@
 def line_kernel(
     rows_ref, inner_ref, outer_ref, out_ref,
     rows, inner, outer, parts, twin_in, cross_out, cross_in, line_out, line_up, line_down,
-    gather_send, gather_recv, twin_send, twin_recv, cross_send, cross_recv,
+    gather_send, gather_recv, twin_send, twin_recv, cross_send, cross_recv, late_out, late_in, late_sem,
     up_send, up_recv, down_send, down_recv, weight_sem,
 ):
     length = 4
@@ -103,6 +103,8 @@
     twin_dev = {"expert": x * 2 + (1 - core)}
     devs = (up_dev, down_dev, cross_dev, twin_dev)
     has_up, has_down = z < length - 1, z > 0
+    at_end = (z == 0) | (z == length - 1)
+    half = tok // 2
     own_slot = core * 2 + x
     cross_slot = core * 2 + (1 - x)
 
@@ -137,9 +139,12 @@
             device_id=devs[way], device_id_type=pl.DeviceIdType.MESH,
         )
 
+    def sem_at(ref, at):
+        return ref.at[at[0], at[1]] if isinstance(at, tuple) else ref.at[at]
+
     def moved(src, dst, send, recv, dev, at):
         return pltpu.make_async_remote_copy(
-            src_ref=src, dst_ref=dst.at[at], send_sem=send.at[at], recv_sem=recv.at[at],
+            src_ref=src, dst_ref=sem_at(dst, at), send_sem=sem_at(send, at), recv_sem=sem_at(recv, at),
             device_id=dev, device_id_type=pl.DeviceIdType.MESH,
         )
 
@@ -149,11 +154,17 @@
     def cross_copy(plane):
         return moved(cross_out.at[plane], cross_in, cross_send, cross_recv, cross_dev, plane)
 
-    def up_copy(plane):
-        return moved(line_out.at[plane], line_up, up_send, up_recv, up_dev, plane)
-
-    def down_copy(plane):
-        return moved(line_out.at[plane], line_down, down_send, down_recv, down_dev, plane)
+    def up_copy(plane, piece):
+        return moved(line_out.at[plane, piece], line_up, up_send, up_recv, up_dev, (plane, piece))
+
+    def down_copy(plane, piece):
+        return moved(line_out.at[plane, piece], line_down, down_send, down_recv, down_dev, (plane, piece))
+
+    def late_copy():
+        return pltpu.make_async_remote_copy(
+            src_ref=late_out, dst_ref=late_in, send_sem=late_sem.at[0], recv_sem=late_sem.at[1],
+            device_id=cross_dev, device_id_type=pl.DeviceIdType.MESH,
+        )
 
     def plane_of(i):
         second = jnp.where(z == 0, 1, z - 1)
@@ -214,11 +225,49 @@
             value = jnp.dot(hidden, outer[:, low:high], preferred_element_type=jnp.float32) * gain
             parts[plane, :, :, low:high] = value.astype(jnp.bfloat16).reshape(4, tok, high - low)
 
+    near, far = slice(0, half), slice(half, tok)
+
+    def pair_sum(plane, slot, source, span):
+        return parts[plane, slot, span].astype(jnp.float32) + twin_in[plane, source, span].astype(jnp.float32)
+
     def cross_sum(plane):
         twin_copy(plane).wait_recv()
-        total = parts[plane, cross_slot].astype(jnp.float32) + twin_in[plane, 1 - x].astype(jnp.float32)
-        cross_out[plane] = total.astype(jnp.bfloat16)
+        cross_out[plane] = pair_sum(plane, cross_slot, 1 - x, near).astype(jnp.bfloat16)
         cross_copy(plane).start()
+
+    def piece_sum(plane, piece):
+        if piece == 1:
+            return pair_sum(plane, cross_slot, 1 - x, far)
+        if piece == 2:
+            return pair_sum(plane, own_slot, x, far)
+        cross_copy(plane).wait_recv()
+        return pair_sum(plane, own_slot, x, near) + cross_in[plane].astype(jnp.float32)
+
+    def line_first(plane, piece):
+        line_out[plane, piece] = piece_sum(plane, piece).astype(jnp.bfloat16)
+
+        @pl.when(z == 0)
+        def _():
+            up_copy(plane, piece).start()
+
+        @pl.when(z == length - 1)
+        def _():
+            down_copy(plane, piece).start()
+
+    def line_next(plane, piece):
+        total = piece_sum(plane, piece)
+
+        @pl.when(plane > z)
+        def _():
+            up_copy(plane, piece).wait_recv()
+            line_out[plane, piece] = (total + line_up[plane, piece].astype(jnp.float32)).astype(jnp.bfloat16)
+            up_copy(plane, piece).start()
+
+        @pl.when(plane < z)
+        def _():
+            down_copy(plane, piece).wait_recv()
+            line_out[plane, piece] = (total + line_down[plane, piece].astype(jnp.float32)).astype(jnp.bfloat16)
+            down_copy(plane, piece).start()
 
     def step(i, carry):
         plane = plane_of(i)
@@ -240,77 +289,66 @@
         expert_part(plane)
         twin_copy(plane).start()
 
-        @pl.when(i >= 1)
-        def _():
-            cross_sum(plane_of(i - 1))
+        cross_sum(plane)
+
+        @pl.when(at_end & (i >= 1))
+        def _():
+            line_first(plane, 1)
+            line_first(plane, 2)
+
+        @pl.when(at_end & (i >= 2))
+        def _():
+            line_first(plane_of(i - 1), 0)
 
         return carry
 
     lax.fori_loop(0, length, step, 0)
-    cross_sum(plane_of(3))
-
-    def column_sum(plane):
-        cross_copy(plane).wait_recv()
-        return (
-            parts[plane, own_slot].astype(jnp.float32)
-            + twin_in[plane, x].astype(jnp.float32)
-            + cross_in[plane].astype(jnp.float32)
-        )
+
+    @pl.when(at_end)
+    def _():
+        line_first(plane_of(length - 1), 0)
 
     def line_step(j, carry):
-        first = jnp.where(z <= 1, z + 1, z - 1)
-        second = jnp.where(z <= 1, z + 2, z - 2)
-        third = jnp.where(z == 0, 3, jnp.where(z == 1, 0, jnp.where(z == 2, 3, 0)))
+        first = jnp.where(z <= 1, 2, 1)
+        second = jnp.where(z <= 1, 3, 0)
+        third = jnp.where(z <= 1, 0, 3)
         plane = jnp.where(j == 0, first, jnp.where(j == 1, second, third))
-        total = column_sum(plane)
-
-        @pl.when(plane > z)
-        def _():
-            @pl.when(has_down)
-            def _():
-                up_copy(plane).wait_recv()
-                line_out[plane] = (total + line_up[plane].astype(jnp.float32)).astype(jnp.bfloat16)
-
-            @pl.when(z == 0)
-            def _():
-                line_out[plane] = total.astype(jnp.bfloat16)
-
-            up_copy(plane).start()
-
-        @pl.when(plane < z)
-        def _():
-            @pl.when(has_up)
-            def _():
-                down_copy(plane).wait_recv()
-                line_out[plane] = (total + line_down[plane].astype(jnp.float32)).astype(jnp.bfloat16)
-
-            @pl.when(z == length - 1)
-            def _():
-                line_out[plane] = total.astype(jnp.bfloat16)
-
-            down_copy(plane).start()
-
+        for piece in (1, 2, 0):
+            line_next(plane, piece)
         return carry
 
-    lax.fori_loop(0, length - 1, line_step, 0)
-    total = column_sum(z)
+    @pl.when(jnp.logical_not(at_end))
+    def _():
+        lax.fori_loop(0, length - 1, line_step, 0)
+
+    def arrived(piece):
+        @pl.when(has_down)
+        def _():
+            up_copy(z, piece).wait_recv()
+
+        @pl.when(has_up)
+        def _():
+            down_copy(z, piece).wait_recv()
+
+        from_below = jnp.where(has_down, line_up[z, piece].astype(jnp.float32), 0.0)
+        from_above = jnp.where(has_up, line_down[z, piece].astype(jnp.float32), 0.0)
+        return piece_sum(z, piece) + from_below + from_above
 
     @pl.when(z == 0)
     def _():
-        down_copy(z).wait_recv()
-        out_ref[...] = (total + line_down[z].astype(jnp.float32)).astype(jnp.bfloat16)
+        line_up[z] = jnp.zeros(line_up.shape[1:], jnp.bfloat16)
 
     @pl.when(z == length - 1)
     def _():
-        up_copy(z).wait_recv()
-        out_ref[...] = (total + line_up[z].astype(jnp.float32)).astype(jnp.bfloat16)
-
-    @pl.when(has_up & has_down)
-    def _():
-        up_copy(z).wait_recv()
-        down_copy(z).wait_recv()
-        both = line_up[z].astype(jnp.float32) + line_down[z].astype(jnp.float32)
-        out_ref[...] = (total + both).astype(jnp.bfloat16)
+        line_down[z] = jnp.zeros(line_down.shape[1:], jnp.bfloat16)
+
+    late_out[...] = arrived(1).astype(jnp.bfloat16)
+    late_copy().start()
+    out_ref[near] = arrived(0).astype(jnp.bfloat16)
+    own = arrived(2)
+    late_copy().wait_recv()
+    out_ref[far] = (own + late_in[...].astype(jnp.float32)).astype(jnp.bfloat16)
+    late_copy().wait_send()
 
     def drain(plane, carry):
         @pl.when(has_up & (plane <= z))
@@ -329,11 +367,13 @@
 
         @pl.when(plane > z)
         def _():
-            up_copy(plane).wait_send()
+            for piece in range(3):
+                up_copy(plane, piece).wait_send()
 
         @pl.when(plane < z)
         def _():
-            down_copy(plane).wait_send()
+            for piece in range(3):
+                down_copy(plane, piece).wait_send()
 
         return carry
 
@@ -356,7 +396,9 @@
     inner = jnp.swapaxes(inner_weight[0], 1, 2)
     bf16 = jnp.bfloat16
     dma = pltpu.SemaphoreType.DMA
-    block = pltpu.VMEM((length, tok, width), bf16)
+    half = tok // 2
+    halves = pltpu.VMEM((length, half, width), bf16)
+    line = pltpu.VMEM((length, 3, half, width), bf16)
     return pl.pallas_call(
         line_kernel,
         out_shape=jax.ShapeDtypeStruct((tok, width), bf16),
@@ -372,10 +414,11 @@
             pltpu.VMEM((hidden, width), bf16),
             pltpu.VMEM((length, 4, tok, width), bf16),
             pltpu.VMEM((length, 2, tok, width), bf16),
-            block, block, block, block, block,
+            halves, halves, line, line, line,
             dma((4, length, 4)), dma((length, 4)),
             dma((length,)), dma((length,)), dma((length,)), dma((length,)),
-            dma((length,)), dma((length,)), dma((length,)), dma((length,)),
+            pltpu.VMEM((half, width), bf16), pltpu.VMEM((half, width), bf16), dma((2,)),
+            dma((length, 3)), dma((length, 3)), dma((length, 3)), dma((length, 3)),
             dma((2,)),
         ],
         compiler_params=pltpu.CompilerParams(
@@ -392,7 +435,7 @@
     four = lax.axis_size("expert") == 4 and lax.axis_size("helper") == 4
     if capacity < tok_count:
         chosen = routed_body
-    elif four and tok_count % 16 == 0 and spare >= 3 * experts_all:
+    elif four and tok_count % 32 == 0 and spare >= 3 * experts_all:
         chosen = line_body
     else:
         chosen = dense_body

time: 107 us -> 99 us (0.925)
  Pallas kernels: 103 us -> 94.4 us
    pallas_call x1, Pallas kernels: 103 us -> 94.4 us  [line_body(): pl.pallas_call(line_kernel, out_shape=jax.ShapeDtypeStruct((tok, width),...]
where the time goes in v3:
time: 99 us; the launch traced here: 98.8 us
  Pallas kernels  94.4 us (95%)
  other arithmetic  2.54 us (3%)
  local copies, waits for them, and re-layouts  1.86 us (2%)
    pallas_call x1, Pallas kernels, line_body(): pl.pallas_call(line_kernel, out_shape=jax.ShapeDtypeStruct((tok, width),...  94.4 us

profile of v3, /device:TPU:0, one launch (start us, length us, event | category | flops | bytes accessed | tf_op | source)
XLA Modules:
  0.0 98.8 jit_solution(7467056923531292021)
XLA Ops:
  0.0 0.7 select_reduce_fusion
  0.7 0.1 copy.11
  0.8 1.8 %fusion.1.rows_ref = bf16[64,2944]{1,0:T(8,128)(2,1)} fusion(bf16[64,24]{1,0:T(8,128)(2,1)S(1)} %copy.11, bf16[64,2880]{1,0:T(8,128)(2,1)} %param.5), kind=kLoop, calls=%fused_computation.2 | loop fusion | flops 1130496 | bytes 748544 | tf_op jit(solution)/shard_map/concatenate | solution.py:395
  2.6 94.4 %shard_map.55 = bf16[64,2880]{1,0:T(8,128)(2,1)} custom-call(bf16[64,2944]{1,0:T(8,128)(2,1)} %fusion.1.rows_ref, bf16[2,720,2880]{2,1,0:T(8,128)(2,1)} %bitcast.4, bf16[720,2880]{1,0:T(8,128)(2,1)} %bitcast.5), custom_call_target="tpu_custom_call" | custom-call | tf_op jit(solution)/shard_map/pallas_call | solution.py:402
  97.0 1.8 %copy.13 = bf16[64,2880]{1,0:T(8,128)(2,1)} copy(bf16[64,2880]{1,0:T(8,128)(2,1)} %shard_map.55) | data formatting | bytes 737280
  (2 shorter events, 0.0 us)

commit v4 on v3

--- a/solution.py
+++ b/solution.py
@@ -105,6 +105,7 @@
     has_up, has_down = z < length - 1, z > 0
     at_end = (z == 0) | (z == length - 1)
     half = tok // 2
+    nearest = jnp.where(z <= 1, 2, 1)
     own_slot = core * 2 + x
     cross_slot = core * 2 + (1 - x)
 
@@ -278,6 +279,12 @@
 
         block_copy(ACROSS, plane, cross_slot).wait_recv()
         block_copy(TWIN, plane, cross_slot).start()
+
+        @pl.when(jnp.logical_not(at_end) & (i == length - 1))
+        def _():
+            line_next(nearest, 1)
+            line_next(nearest, 2)
+
         for other in range(2):
             block_copy(TWIN, plane, (1 - core) * 2 + other).wait_recv()
 
@@ -289,7 +296,9 @@
         expert_part(plane)
         twin_copy(plane).start()
 
-        cross_sum(plane)
+        @pl.when(i >= 1)
+        def _():
+            cross_sum(plane)
 
         @pl.when(at_end & (i >= 1))
         def _():
@@ -303,23 +312,22 @@
         return carry
 
     lax.fori_loop(0, length, step, 0)
+    cross_sum(z)
 
     @pl.when(at_end)
     def _():
         line_first(plane_of(length - 1), 0)
 
     def line_step(j, carry):
-        first = jnp.where(z <= 1, 2, 1)
-        second = jnp.where(z <= 1, 3, 0)
-        third = jnp.where(z <= 1, 0, 3)
-        plane = jnp.where(j == 0, first, jnp.where(j == 1, second, third))
+        plane = jnp.where((z <= 1) == (j == 0), 3, 0)
         for piece in (1, 2, 0):
             line_next(plane, piece)
         return carry
 
     @pl.when(jnp.logical_not(at_end))
     def _():
-        lax.fori_loop(0, length - 1, line_step, 0)
+        line_next(nearest, 0)
+        lax.fori_loop(0, 2, line_step, 0)
 
     def arrived(piece):
         @pl.when(has_down)

time: 99 us -> 95.9 us (0.969)
  Pallas kernels: 94.4 us -> 91.2 us
    pallas_call x1, Pallas kernels: 94.4 us -> 91.2 us  [line_body(): pl.pallas_call(line_kernel, out_shape=jax.ShapeDtypeStruct((tok, width),...]
where the time goes in v4:
time: 95.9 us; the launch traced here: 95.6 us
  Pallas kernels  91.2 us (95%)
  other arithmetic  2.54 us (3%)
  local copies, waits for them, and re-layouts  1.86 us (2%)
    pallas_call x1, Pallas kernels, line_body(): pl.pallas_call(line_kernel, out_shape=jax.ShapeDtypeStruct((tok, width),...  91.2 us

profile of v4, /device:TPU:0, one launch (start us, length us, event | category | flops | bytes accessed | tf_op | source)
XLA Modules:
  0.0 95.6 jit_solution(758852806262531438)
XLA Ops:
  0.0 0.7 select_reduce_fusion
  0.7 0.1 copy.11
  0.8 1.8 %fusion.1.rows_ref = bf16[64,2944]{1,0:T(8,128)(2,1)} fusion(bf16[64,24]{1,0:T(8,128)(2,1)S(1)} %copy.11, bf16[64,2880]{1,0:T(8,128)(2,1)} %param.5), kind=kLoop, calls=%fused_computation.2 | loop fusion | flops 1130496 | bytes 748544 | tf_op jit(solution)/shard_map/concatenate | solution.py:403
  2.6 91.2 %shard_map.55 = bf16[64,2880]{1,0:T(8,128)(2,1)} custom-call(bf16[64,2944]{1,0:T(8,128)(2,1)} %fusion.1.rows_ref, bf16[2,720,2880]{2,1,0:T(8,128)(2,1)} %bitcast.4, bf16[720,2880]{1,0:T(8,128)(2,1)} %bitcast.5), custom_call_target="tpu_custom_call" | custom-call | tf_op jit(solution)/shard_map/pallas_call | solution.py:410
  93.9 1.8 %copy.13 = bf16[64,2880]{1,0:T(8,128)(2,1)} copy(bf16[64,2880]{1,0:T(8,128)(2,1)} %shard_map.55) | data formatting | bytes 737280
  (2 shorter events, 0.0 us)

commit v5 on v4

--- a/solution.py
+++ b/solution.py
@@ -87,6 +87,7 @@
     rows_ref, inner_ref, outer_ref, out_ref,
     rows, inner, outer, parts, twin_in, cross_out, cross_in, line_out, line_up, line_down,
     gather_send, gather_recv, twin_send, twin_recv, cross_send, cross_recv, late_out, late_in, late_sem,
+    tail_send, tail_recv,
     up_send, up_recv, down_send, down_recv, weight_sem,
 ):
     length = 4
@@ -143,6 +144,22 @@
     def sem_at(ref, at):
         return ref.at[at[0], at[1]] if isinstance(at, tuple) else ref.at[at]
 
+    main = tok - 16
+
+    def main_copy(plane, slot):
+        return pltpu.make_async_remote_copy(
+            src_ref=rows.at[plane, slot, pl.ds(0, main)], dst_ref=rows.at[plane, slot, pl.ds(0, main)],
+            send_sem=gather_send.at[ACROSS, plane, slot], recv_sem=gather_recv.at[plane, slot],
+            device_id=cross_dev, device_id_type=pl.DeviceIdType.MESH,
+        )
+
+    def tail_copy(way, plane, slot):
+        return pltpu.make_async_remote_copy(
+            src_ref=rows.at[plane, slot, pl.ds(main, 16)], dst_ref=rows.at[plane, slot, pl.ds(main, 16)],
+            send_sem=tail_send.at[way, plane], recv_sem=tail_recv.at[plane],
+            device_id=devs[way], device_id_type=pl.DeviceIdType.MESH,
+        )
+
     def moved(src, dst, send, recv, dev, at):
         return pltpu.make_async_remote_copy(
             src_ref=src, dst_ref=sem_at(dst, at), send_sem=sem_at(send, at), recv_sem=sem_at(recv, at),
@@ -181,8 +198,18 @@
     def _():
         block_copy(DOWN, z, own_slot).start()
 
-    block_copy(ACROSS, z, own_slot).start()
+    tail_copy(ACROSS, z, own_slot).start()
+    main_copy(z, own_slot).start()
     block_copy(TWIN, z, own_slot).start()
+    tail_copy(ACROSS, z, cross_slot).wait_recv()
+
+    @pl.when(has_up)
+    def _():
+        tail_copy(UP, z, cross_slot).start()
+
+    @pl.when(has_down)
+    def _():
+        tail_copy(DOWN, z, cross_slot).start()
 
     def shift_in(dist):
         @pl.when(z - dist >= 0)
@@ -194,8 +221,13 @@
             def _():
                 block_copy(UP, plane, own_slot).start()
 
-            block_copy(ACROSS, plane, own_slot).start()
+            main_copy(plane, own_slot).start()
             block_copy(TWIN, plane, own_slot).start()
+            tail_copy(UP, plane, cross_slot).wait_recv()
+
+            @pl.when(has_up)
+            def _():
+                tail_copy(UP, plane, cross_slot).start()
 
         @pl.when(z + dist <= length - 1)
         def _():
@@ -206,8 +238,13 @@
             def _():
                 block_copy(DOWN, plane, own_slot).start()
 
-            block_copy(ACROSS, plane, own_slot).start()
+            main_copy(plane, own_slot).start()
             block_copy(TWIN, plane, own_slot).start()
+            tail_copy(DOWN, plane, cross_slot).wait_recv()
+
+            @pl.when(has_down)
+            def _():
+                tail_copy(DOWN, plane, cross_slot).start()
 
     def expert_part(plane):
         group = rows[plane].reshape(4 * tok, rows_ref.shape[1])
@@ -277,7 +314,7 @@
         def _():
             shift_in(i + 1)
 
-        block_copy(ACROSS, plane, cross_slot).wait_recv()
+        main_copy(plane, cross_slot).wait_recv()
         block_copy(TWIN, plane, cross_slot).start()
 
         @pl.when(jnp.logical_not(at_end) & (i == length - 1))
@@ -367,7 +404,16 @@
         def _():
             block_copy(DOWN, plane, own_slot).wait_send()
 
-        block_copy(ACROSS, plane, own_slot).wait_send()
+        main_copy(plane, own_slot).wait_send()
+
+        @pl.when(has_up & (plane <= z))
+        def _():
+            tail_copy(UP, plane, cross_slot).wait_send()
+
+        @pl.when(has_down & (plane >= z))
+        def _():
+            tail_copy(DOWN, plane, cross_slot).wait_send()
+
         block_copy(TWIN, plane, own_slot).wait_send()
         block_copy(TWIN, plane, cross_slot).wait_send()
         twin_copy(plane).wait_send()
@@ -386,6 +432,7 @@
         return carry
 
     lax.fori_loop(0, length, drain, 0)
+    tail_copy(ACROSS, z, own_slot).wait_send()
 
 
 def line_body(activations, expert_ids, route_gates, inner_weight, outer_weight):
@@ -426,6 +473,7 @@
             dma((4, length, 4)), dma((length, 4)),
             dma((length,)), dma((length,)), dma((length,)), dma((length,)),
             pltpu.VMEM((half, width), bf16), pltpu.VMEM((half, width), bf16), dma((2,)),
+            dma((3, length)), dma((length,)),
             dma((length, 3)), dma((length, 3)), dma((length, 3)), dma((length, 3)),
             dma((2,)),
         ],

time: 95.9 us -> 99.7 us (1.040)
  Pallas kernels: 91.2 us -> 95 us
    pallas_call x1, Pallas kernels: 91.2 us -> 95 us  [line_body(): pl.pallas_call(line_kernel, out_shape=jax.ShapeDtypeStruct((tok, width),...]
where the time goes in v5:
time: 99.7 us; the launch traced here: 99.4 us
  Pallas kernels  95 us (95%)
  other arithmetic  2.54 us (3%)
  local copies, waits for them, and re-layouts  1.86 us (2%)
    pallas_call x1, Pallas kernels, line_body(): pl.pallas_call(line_kernel, out_shape=jax.ShapeDtypeStruct((tok, width),...  95 us

profile of v5, /device:TPU:0, one launch (start us, length us, event | category | flops | bytes accessed | tf_op | source)
XLA Modules:
  0.0 99.4 jit_solution(12341636206329648396)
XLA Ops:
  0.0 0.7 select_reduce_fusion
  0.7 0.1 copy.11
  0.8 1.8 %fusion.1.rows_ref = bf16[64,2944]{1,0:T(8,128)(2,1)} fusion(bf16[64,24]{1,0:T(8,128)(2,1)S(1)} %copy.11, bf16[64,2880]{1,0:T(8,128)(2,1)} %param.5), kind=kLoop, calls=%fused_computation.2 | loop fusion | flops 1130496 | bytes 748544 | tf_op jit(solution)/shard_map/concatenate | solution.py:450
  2.6 95.0 %shard_map.55 = bf16[64,2880]{1,0:T(8,128)(2,1)} custom-call(bf16[64,2944]{1,0:T(8,128)(2,1)} %fusion.1.rows_ref, bf16[2,720,2880]{2,1,0:T(8,128)(2,1)} %bitcast.4, bf16[720,2880]{1,0:T(8,128)(2,1)} %bitcast.5), custom_call_target="tpu_custom_call" | custom-call | tf_op jit(solution)/shard_map/pallas_call | solution.py:457
  97.6 1.8 %copy.13 = bf16[64,2880]{1,0:T(8,128)(2,1)} copy(bf16[64,2880]{1,0:T(8,128)(2,1)} %shard_map.55) | data formatting | bytes 737280
  (2 shorter events, 0.0 us)

commit v6 on v4

--- a/solution.py
+++ b/solution.py
@@ -104,7 +104,7 @@
     devs = (up_dev, down_dev, cross_dev, twin_dev)
     has_up, has_down = z < length - 1, z > 0
     at_end = (z == 0) | (z == length - 1)
-    half = tok // 2
+    half = tok - 16
     nearest = jnp.where(z <= 1, 2, 1)
     own_slot = core * 2 + x
     cross_slot = core * 2 + (1 - x)
@@ -155,11 +155,21 @@
     def cross_copy(plane):
         return moved(cross_out.at[plane], cross_in, cross_send, cross_recv, cross_dev, plane)
 
+    def span(piece):
+        return pl.ds(0, tok - half if piece else half)
+
+    def line_copy(src, dst, send, recv, dev, plane, piece):
+        return pltpu.make_async_remote_copy(
+            src_ref=src.at[plane, piece, span(piece)], dst_ref=dst.at[plane, piece, span(piece)],
+            send_sem=send.at[plane, piece], recv_sem=recv.at[plane, piece],
+            device_id=dev, device_id_type=pl.DeviceIdType.MESH,
+        )
+
     def up_copy(plane, piece):
-        return moved(line_out.at[plane, piece], line_up, up_send, up_recv, up_dev, (plane, piece))
+        return line_copy(line_out, line_up, up_send, up_recv, up_dev, plane, piece)
 
     def down_copy(plane, piece):
-        return moved(line_out.at[plane, piece], line_down, down_send, down_recv, down_dev, (plane, piece))
+        return line_copy(line_out, line_down, down_send, down_recv, down_dev, plane, piece)
 
     def late_copy():
         return pltpu.make_async_remote_copy(
@@ -245,7 +255,7 @@
         return pair_sum(plane, own_slot, x, near) + cross_in[plane].astype(jnp.float32)
 
     def line_first(plane, piece):
-        line_out[plane, piece] = piece_sum(plane, piece).astype(jnp.bfloat16)
+        line_out[plane, piece, span(piece)] = piece_sum(plane, piece).astype(jnp.bfloat16)
 
         @pl.when(z == 0)
         def _():
@@ -261,13 +271,13 @@
         @pl.when(plane > z)
         def _():
             up_copy(plane, piece).wait_recv()
-            line_out[plane, piece] = (total + line_up[plane, piece].astype(jnp.float32)).astype(jnp.bfloat16)
+            line_out[plane, piece, span(piece)] = (total + line_up[plane, piece, span(piece)].astype(jnp.float32)).astype(jnp.bfloat16)
             up_copy(plane, piece).start()
 
         @pl.when(plane < z)
         def _():
             down_copy(plane, piece).wait_recv()
-            line_out[plane, piece] = (total + line_down[plane, piece].astype(jnp.float32)).astype(jnp.bfloat16)
+            line_out[plane, piece, span(piece)] = (total + line_down[plane, piece, span(piece)].astype(jnp.float32)).astype(jnp.bfloat16)
             down_copy(plane, piece).start()
 
     def step(i, carry):
@@ -338,8 +348,8 @@
         def _():
             down_copy(z, piece).wait_recv()
 
-        from_below = jnp.where(has_down, line_up[z, piece].astype(jnp.float32), 0.0)
-        from_above = jnp.where(has_up, line_down[z, piece].astype(jnp.float32), 0.0)
+        from_below = jnp.where(has_down, line_up[z, piece, span(piece)].astype(jnp.float32), 0.0)
+        from_above = jnp.where(has_up, line_down[z, piece, span(piece)].astype(jnp.float32), 0.0)
         return piece_sum(z, piece) + from_below + from_above
 
     @pl.when(z == 0)
@@ -404,7 +414,7 @@
     inner = jnp.swapaxes(inner_weight[0], 1, 2)
     bf16 = jnp.bfloat16
     dma = pltpu.SemaphoreType.DMA
-    half = tok // 2
+    half = tok - 16
     halves = pltpu.VMEM((length, half, width), bf16)
     line = pltpu.VMEM((length, 3, half, width), bf16)
     return pl.pallas_call(
@@ -425,7 +435,7 @@
             halves, halves, line, line, line,
             dma((4, length, 4)), dma((length, 4)),
             dma((length,)), dma((length,)), dma((length,)), dma((length,)),
-            pltpu.VMEM((half, width), bf16), pltpu.VMEM((half, width), bf16), dma((2,)),
+            pltpu.VMEM((tok - half, width), bf16), pltpu.VMEM((tok - half, width), bf16), dma((2,)),
             dma((length, 3)), dma((length, 3)), dma((length, 3)), dma((length, 3)),
             dma((2,)),
         ],

time: 95.9 us -> 96.1 us (level)
  no operation moved by 1% of the time
where the time goes in v6:
time: 96.1 us; the launch traced here: 95.8 us
  Pallas kernels  91.4 us (95%)
  other arithmetic  2.54 us (3%)
  local copies, waits for them, and re-layouts  1.86 us (2%)
    pallas_call x1, Pallas kernels, line_body(): pl.pallas_call(line_kernel, out_shape=jax.ShapeDtypeStruct((tok, width),...  91.4 us

profile of v6, /device:TPU:0, one launch (start us, length us, event | category | flops | bytes accessed | tf_op | source)
XLA Modules:
  0.0 95.8 jit_solution(11799575630571839540)
XLA Ops:
  0.0 0.7 select_reduce_fusion
  0.7 0.1 copy.11
  0.8 1.8 %fusion.1.rows_ref = bf16[64,2944]{1,0:T(8,128)(2,1)} fusion(bf16[64,24]{1,0:T(8,128)(2,1)S(1)} %copy.11, bf16[64,2880]{1,0:T(8,128)(2,1)} %param.5), kind=kLoop, calls=%fused_computation.2 | loop fusion | flops 1130496 | bytes 748544 | tf_op jit(solution)/shard_map/concatenate | solution.py:413
  2.6 91.4 %shard_map.55 = bf16[64,2880]{1,0:T(8,128)(2,1)} custom-call(bf16[64,2944]{1,0:T(8,128)(2,1)} %fusion.1.rows_ref, bf16[2,720,2880]{2,1,0:T(8,128)(2,1)} %bitcast.4, bf16[720,2880]{1,0:T(8,128)(2,1)} %bitcast.5), custom_call_target="tpu_custom_call" | custom-call | tf_op jit(solution)/shard_map/pallas_call | solution.py:420
  94.1 1.8 %copy.13 = bf16[64,2880]{1,0:T(8,128)(2,1)} copy(bf16[64,2880]{1,0:T(8,128)(2,1)} %shard_map.55) | data formatting | bytes 737280
  (2 shorter events, 0.0 us)
